TPU v7x, 32 devices: a whole 2x2x4 slice. The times are simulated.
32 devices in a mesh: fsdp: 8 (over z, y), ctx: 2 (over core), tp: 2 (over x).
Axes of the slice: x: 2, y: 2, z: 4, core: 2. Of those that a mesh axis runs over, the one named last changes fastest.
Arguments:
- image: float32 [8, 56, 56, 512], P('fsdp', 'ctx', 'tp'), may hold values from -6 to 6
- cotangent: float32 [8, 56, 56, 512], P('fsdp', 'ctx', 'tp'), may hold values from -6 to 6
- norm_gain: bfloat16 [2, 512], P(None, ('fsdp', 'ctx')), may hold values from 0.25 to 1.75
- norm_bias: bfloat16 [2, 512], P(None, ('fsdp', 'ctx')), may hold values from -1.75 to 1.75
- qkv_weight: bfloat16 [512, 3, 512], P(('fsdp', 'ctx'), None, 'tp'), may hold values from -2 to 2
- qkv_bias: bfloat16 [2, 512], P(None, 'tp'), may hold values from -3 to 3
- bias_table: bfloat16 [16, 169], P('tp'), may hold values from -6 to 6
- bias_index: int32 [49, 49], replicated, may hold values from 0 to 168
- regions: int32 [56, 56], P('ctx'), may hold values from 0 to 8, as said below
- proj_weight: bfloat16 [512, 512], P('tp', ('fsdp', 'ctx')), may hold values from -1 to 1
- out_bias: bfloat16 [2, 512], P(None, ('fsdp', 'ctx')), may hold values from -1.75 to 1.75
- up_weight: bfloat16 [512, 2048], P(('fsdp', 'ctx'), 'tp'), may hold values from -0.25 to 0.25
- up_bias: bfloat16 [2048], P('tp'), may hold values from -3 to 3
- down_weight: bfloat16 [2048, 512], P('tp', ('fsdp', 'ctx')), may hold values from -0.1875 to 0.1875
Outputs:
- output: float32 [8, 56, 56, 512], P('fsdp', 'ctx', 'tp')
- image_grad: float32 [8, 56, 56, 512], P('fsdp', 'ctx', 'tp')
- norm_gain_grad: float32 [2, 512], P(None, ('fsdp', 'ctx'))
- norm_bias_grad: float32 [2, 512], P(None, ('fsdp', 'ctx'))
- qkv_weight_grad: float32 [512, 3, 512], P(('fsdp', 'ctx'), None, 'tp')
- qkv_bias_grad: float32 [2, 512], P(None, 'tp')
- bias_table_grad: float32 [16, 169], P('tp')
- proj_weight_grad: float32 [512, 512], P('tp', ('fsdp', 'ctx'))
- out_bias_grad: float32 [2, 512], P(None, ('fsdp', 'ctx'))
- up_weight_grad: float32 [512, 2048], P(('fsdp', 'ctx'), 'tp')
- up_bias_grad: float32 [2048], P('tp')
- down_weight_grad: float32 [2048, 512], P('tp', ('fsdp', 'ctx'))
Inputs may be any that keep to these rules, and one draw needn't show every extreme that they name: `bias_index`: for each query position and key position of a window, the row of bias_table that holds their bias. `regions`: 3 times a row label plus a column label; each label counts how many of two boundaries near the end of the grid the row or column has passed.
All inputs are finite; a program needn't handle non-finite values.
Results may differ from a plain program's by a relative error of at most 0.015.
Values may be sent and summed in bfloat16 or wider, within the bound.
A program may use at most 192 MiB of HBM per device.

v0:
```python
import math

import jax
import jax.numpy as jnp
from jax import lax
from jax.experimental import pallas as pl
from jax.experimental.pallas import tpu as pltpu
from jax.sharding import PartitionSpec as P

HEAD_DIM = 32
WIN = 7
PAD = 8
AREA = PAD * PAD
SHIFT = 3
GROUP = 8
LANES = GROUP * HEAD_DIM
TALL = GROUP * AREA
PER_STEP = 4
ROWS = PER_STEP * AREA

EPSILON = 1e-05
MASKED = -100.0
ABSENT = -1e30
SCALE = 1.0 / math.sqrt(HEAD_DIM)
F32 = jnp.float32
BF16 = jnp.bfloat16


def shifted(value, axis, steps):
    count = lax.axis_size(axis)
    pairs = [(source, (source + steps) % count) for source in range(count)]
    return lax.ppermute(value, axis, pairs)


def bits(axis):
    return [1 << k for k in range(lax.axis_size(axis).bit_length() - 1)]


def swap(value, axis, bit):
    return lax.ppermute(value, axis, [(i, i ^ bit) for i in range(lax.axis_size(axis))])


def own_bit(axis, bit):
    return (lax.axis_index(axis) // bit) % 2


def split_bits():
    high_first = bits("fsdp")[::-1]
    cut = len(high_first) - len(high_first) // 3
    return [("fsdp", bit) for bit in high_first[:cut]], [("fsdp", bit) for bit in high_first[cut:]]


def gather_steps(held, order):
    for axis, bit in order:
        other = swap(held, axis, bit)
        mine = own_bit(axis, bit)
        low = jnp.where(mine == 0, held, other)
        high = jnp.where(mine == 0, other, held)
        if axis == "tp":
            held = jnp.concatenate([low, high], axis=-1)
        else:
            held = jnp.stack([low, high], axis=held.ndim - 2)
    return held


def first_halves(grads):
    lead, rows_all, cols_all = grads[0].shape
    span = lax.axis_size("fsdp")
    pair = lax.axis_size("ctx")
    rows = rows_all // (span * pair)
    mine = lax.axis_index("ctx")
    cut = lambda g, which: lax.dynamic_index_in_dim(
        g.reshape(lead, span, pair, rows, cols_all), which, 2, keepdims=False
    )
    pick = lambda which: sum(cut(g, which) for g in grads)
    return pick(1 - mine).astype(BF16), pick(mine)


def joined(send, keep, axis, bit):
    return keep + swap(send, axis, bit).astype(F32)


def halves(total, axis, bit, used):
    mine = own_bit(axis, bit)
    if axis == "tp":
        half = total.shape[-1] // 2
        cut = lambda which: lax.dynamic_slice_in_dim(total, which * half, half, 3)
    else:
        lead, span, rows_here, cols_here = total.shape
        low = 1
        for other_bit in bits("fsdp"):
            if other_bit < bit and other_bit not in used:
                low *= 2
        view = total.reshape(lead, span // (2 * low), 2, low, rows_here, cols_here)
        cut = lambda which: lax.dynamic_index_in_dim(view, which, 2, keepdims=False).reshape(
            lead, span // 2, rows_here, cols_here
        )
    return cut(1 - mine).astype(BF16), cut(mine)


def scatter_steps(total, order, used):
    used = set(used)
    for axis, bit in order:
        total = joined(*halves(total, axis, bit, used), axis, bit)
        if axis == "fsdp":
            used.add(bit)
    return total


def layer_stats(values_in):
    mean_row = jnp.mean(values_in, axis=-1, keepdims=True)
    centered = values_in - mean_row
    inverse = lax.rsqrt(jnp.mean(centered * centered, axis=-1, keepdims=True) + EPSILON)
    return (centered * inverse, inverse)


def layer_back(grad_out, normed, inverse, gain_row):
    scaled = grad_out * gain_row
    return inverse * (
        scaled
        - jnp.mean(scaled, axis=-1, keepdims=True)
        - normed * jnp.mean(scaled * normed, axis=-1, keepdims=True)
    )


def mm(left, right, left_dim, right_dim):
    return lax.dot_general(
        left, right, (((left_dim,), (right_dim,)), ((), ())), preferred_element_type=F32
    )


def head_select():
    row = lax.broadcasted_iota(jnp.int32, (TALL, LANES), 0) // AREA
    lane = lax.broadcasted_iota(jnp.int32, (TALL, LANES), 1) // HEAD_DIM
    return (row == lane).astype(F32)


def spread(value, select):
    return jnp.concatenate([value] * GROUP, axis=0) * select


def fold(tall, select):
    return jnp.sum((tall * select).reshape(GROUP, AREA, LANES), axis=0)


def forward_kernel(
    x_ref, vec_ref, w_ref, bias_ref, mask_ref, *rest
):
    tok_ref, q_ref, k_ref, v_ref, p_ref, att_ref, mid_ref, n2_ref = rest[-8:]
    vec = vec_ref[...]
    resid = x_ref[...]
    norm, _ = layer_stats(resid)
    tok = (norm * vec[0:1] + vec[2:3]).astype(BF16)
    tok_ref[...] = tok
    q_ref[...] = (mm(tok, w_ref[0], 1, 0) + vec[6:7]).astype(BF16)
    k_ref[...] = mm(tok, w_ref[1], 1, 0).astype(BF16)
    v_ref[...] = (mm(tok, w_ref[2], 1, 0) + vec[7:8]).astype(BF16)
    select = head_select()
    select_half = select.astype(BF16)

    def window(w, carry):
        here = pl.ds(pl.multiple_of(w * AREA, AREA), AREA)
        mask = mask_ref[w]
        mask_tall = jnp.concatenate([mask] * GROUP, axis=0)
        for g in range(w_ref.shape[2] // LANES):
            part = slice(g * LANES, (g + 1) * LANES)
            tall_q = spread(q_ref[here, part], select_half)
            scores = mm(tall_q, k_ref[here, part], 1, 1) * SCALE
            scores = scores + bias_ref[g * TALL : (g + 1) * TALL, :] + mask_tall
            peak = jnp.max(scores, axis=-1, keepdims=True)
            weight = jnp.exp(scores - peak)
            prob = weight / jnp.sum(weight, axis=-1, keepdims=True)
            p_ref[w, g] = prob
            att_ref[here, part] = fold(
                mm(prob.astype(BF16), v_ref[here, part], 1, 0), select
            ).astype(BF16)
        return carry

    lax.fori_loop(0, PER_STEP, window, 0, unroll=True)
    middle = resid + mm(att_ref[...], w_ref[3], 1, 1) + vec[4:5]
    mid_ref[...] = middle
    norm_two, _ = layer_stats(middle)
    n2_ref[...] = (norm_two * vec[1:2] + vec[3:4]).astype(BF16)


def ffn_kernel(
    mid_ref, n2_ref, cot_ref, up_ref, down_ref, upb_ref, vec_ref,
    out_ref, gm_ref, dffn_ref, dupb_ref, sums_ref, acc_ref, g2_ref
):
    @pl.when(pl.program_id(0) == 0)
    def _():
        dffn_ref[...] = jnp.zeros_like(dffn_ref)
        dupb_ref[...] = jnp.zeros_like(dupb_ref)
        sums_ref[...] = jnp.zeros_like(sums_ref)

    vec = vec_ref[...]
    chunk = 512
    acc_ref[...] = jnp.zeros_like(acc_ref)
    g2_ref[...] = jnp.zeros_like(g2_ref)

    def step(f, carry):
        here = pl.ds(pl.multiple_of(f * chunk, chunk), chunk)
        rows_two = n2_ref[...]
        cot_half = cot_ref[...].astype(BF16)
        pre = mm(rows_two, up_ref[:, here], 1, 0) + upb_ref[:, here]
        phi = 0.5 * (1.0 + lax.erf(pre * (1.0 / math.sqrt(2.0))))
        hidden = (pre * phi).astype(BF16)
        slope = mm(cot_half, down_ref[:, here], 1, 0) * (
            phi + pre * jnp.exp(-0.5 * pre * pre) * (1.0 / math.sqrt(2.0 * math.pi))
        )
        slope_half = slope.astype(BF16)
        acc_ref[...] += mm(hidden, down_ref[:, here], 1, 1)
        g2_ref[...] += mm(slope_half, up_ref[:, here], 1, 1)
        dffn_ref[0, :, here] += mm(rows_two, slope_half, 0, 0)
        dffn_ref[1, :, here] += mm(cot_half, hidden, 0, 0)
        dupb_ref[:, here] += jnp.sum(slope, axis=0, keepdims=True)
        return carry

    lax.fori_loop(0, up_ref.shape[1] // chunk, step, 0)
    middle = mid_ref[...]
    cot = cot_ref[...]
    out_ref[...] = middle + acc_ref[...] + vec[5:6]
    norm_two, inv_two = layer_stats(middle)
    grad_two = g2_ref[...]
    grad_mid = cot + layer_back(grad_two, norm_two, inv_two, vec[1:2])
    gm_ref[...] = grad_mid
    total = lambda value: jnp.sum(value, axis=0, keepdims=True)
    sums_ref[0:1] += total(grad_two * norm_two)
    sums_ref[1:2] += total(grad_two)
    sums_ref[2:3] += total(grad_mid)
    sums_ref[3:4] += total(cot)


def backward_kernel(
    x_ref, gm_ref, tok_ref, q_ref, k_ref, v_ref, p_ref, att_ref, w_ref, vec_ref, *rest
):
    img_ref, dw_ref, ds_ref, sums_ref, ga_ref, mixed_ref = rest[-6:]

    @pl.when(pl.program_id(0) == 0)
    def _():
        dw_ref[...] = jnp.zeros_like(dw_ref)
        ds_ref[...] = jnp.zeros_like(ds_ref)
        sums_ref[...] = jnp.zeros_like(sums_ref)

    vec = vec_ref[...]
    grad_mid = gm_ref[...]
    grad_tok = grad_mid.astype(BF16)
    ga_ref[...] = mm(grad_tok, w_ref[3], 1, 0).astype(BF16)
    dw_ref[3] += mm(grad_tok, att_ref[...], 0, 0)
    select = head_select()
    select_half = select.astype(BF16)
    total = lambda value: jnp.sum(value, axis=0, keepdims=True)

    def window(w, carry):
        here = pl.ds(pl.multiple_of(w * AREA, AREA), AREA)
        for g in range(w_ref.shape[2] // LANES):
            part = slice(g * LANES, (g + 1) * LANES)
            tall_q = spread(q_ref[here, part], select_half)
            tall_ga = spread(ga_ref[here, part], select_half)
            prob = p_ref[w, g]
            grad_prob = mm(tall_ga, v_ref[here, part], 1, 1)
            grad_value = mm(prob.astype(BF16), tall_ga, 0, 0)
            weighted = prob * grad_prob
            grad_score = weighted - prob * jnp.sum(weighted, axis=-1, keepdims=True)
            ds_ref[g * TALL : (g + 1) * TALL, :] += grad_score
            score_half = (grad_score * SCALE).astype(BF16)
            grad_query = fold(mm(score_half, k_ref[here, part], 1, 0), select)
            grad_key = mm(score_half, tall_q, 0, 0)
            sums_ref[0:1, part] += total(grad_query)
            sums_ref[1:2, part] += total(grad_value)
            mixed_ref[0, here, part] = grad_query.astype(BF16)
            mixed_ref[1, here, part] = grad_key.astype(BF16)
            mixed_ref[2, here, part] = grad_value.astype(BF16)
        return carry

    lax.fori_loop(0, PER_STEP, window, 0, unroll=True)
    tok = tok_ref[...]
    grad_one = jnp.zeros(grad_mid.shape, F32)
    for j in range(3):
        dw_ref[j] += mm(tok, mixed_ref[j], 0, 0)
        grad_one = grad_one + mm(mixed_ref[j], w_ref[j], 1, 1)
    norm, inv = layer_stats(x_ref[...])
    img_ref[...] = grad_mid + layer_back(grad_one, norm, inv, vec[0:1])
    sums_ref[2:3] += total(grad_one * norm)
    sums_ref[3:4] += total(grad_one)


def to_padded(field):
    images, rows, cols = field.shape[:3]
    rest = field.shape[3:]
    cut = field.reshape(images, rows // WIN, WIN, cols // WIN, WIN, *rest)
    grow = PAD - WIN
    cut = jnp.pad(cut, ((0, 0), (0, 0), (0, grow), (0, 0), (0, grow)) + ((0, 0),) * len(rest))
    order = (0, 1, 3, 2, 4) + tuple(range(5, 5 + len(rest)))
    return cut.transpose(order).reshape(-1, *rest)


def from_padded(tiles, images, rows, cols):
    width = tiles.shape[-1]
    cut = tiles.reshape(images, rows // WIN, cols // WIN, PAD, PAD, width)
    cut = cut.transpose(0, 1, 3, 2, 4, 5)[:, :, :WIN, :, :WIN]
    return cut.reshape(images, rows, cols, width)


def whole_spec(shape):
    return pl.BlockSpec(shape, lambda i: (0,) * len(shape))


def row_spec(cols, first=0):
    return pl.BlockSpec((ROWS, cols), lambda i: (i + first, 0))


PARAMS = dict(compiler_params=pltpu.CompilerParams(vmem_limit_bytes=60 * 1024 * 1024))


def per_device(
    image, cotangent, norm_gain, norm_bias, qkv_weight, qkv_bias, bias_table, bias_index,
    regions, proj_weight, out_bias, up_weight, up_bias, down_weight,
):
    images, band_rows, columns, channels = image.shape
    groups = lax.axis_size("tp")
    table_rows = bias_table.shape[1]
    head_width = qkv_weight.shape[2]
    heads_here = bias_table.shape[0]
    ffn_here = up_bias.shape[0]
    rows_here = qkv_weight.shape[0]

    shards = lax.axis_size("fsdp") * lax.axis_size("ctx")
    small_parts = [
        norm_gain.reshape(-1), norm_bias.reshape(-1), out_bias.reshape(-1), qkv_bias.reshape(-1),
        up_bias, bias_table.reshape(-1),
    ]
    small_len = sum(part.shape[0] for part in small_parts)
    small_rows = -(-small_len // (16 * head_width)) * 16
    small_parts.append(jnp.zeros((small_rows * head_width - small_len,), BF16))
    attn_block = jnp.concatenate(
        [
            qkv_weight[:, 0], qkv_weight[:, 1], qkv_weight[:, 2], proj_weight.T,
            jnp.concatenate(small_parts).reshape(small_rows, head_width),
        ],
        axis=0,
    )
    ffn_block = jnp.stack([up_weight, down_weight.T])
    far, near = split_bits()
    across = [("tp", bit) for bit in bits("tp")]
    last = [("ctx", bit) for bit in bits("ctx")[::-1]]
    attn_all = gather_steps(attn_block, far + near + across + last)
    attn_all = attn_all.reshape(shards, 4 * rows_here + small_rows, groups * head_width)
    attn_w = (
        attn_all[:, : 4 * rows_here]
        .reshape(shards, 4, rows_here, channels)
        .transpose(1, 0, 2, 3)
        .reshape(4, channels, channels)
    )
    ffn_far = gather_steps(ffn_block, far)
    up_held = gather_steps(ffn_far[0], across)
    down_held = gather_steps(ffn_far[1], near)
    up_held, down_held, attn_w = lax.optimization_barrier((up_held, down_held, attn_w))
    up_held = gather_steps(up_held, near)
    down_held = gather_steps(down_held, across)

    small = (
        attn_all[:, 4 * rows_here :]
        .reshape(shards, small_rows, groups, head_width)
        .transpose(0, 2, 1, 3)
        .reshape(shards, groups, -1)
    )
    v_end = 6 * rows_here
    vec_six = (
        small[:, 0, :v_end].reshape(shards, 6, rows_here).transpose(1, 0, 2).reshape(6, channels)
    ).astype(F32)
    small = small[0, :, v_end:small_len]
    qb_end = 2 * head_width
    pair_whole = (
        small[:, :qb_end].reshape(groups, 2, head_width).transpose(1, 0, 2).reshape(2, -1).astype(F32)
    )
    upb_whole = small[:, qb_end : qb_end + ffn_here].reshape(1, -1).astype(F32)
    table_whole = small[:, qb_end + ffn_here :].reshape(groups * heads_here, table_rows)
    vec = jnp.concatenate([vec_six, pair_whole], axis=0)

    edge_image, edge_grad = shifted((image[:, :SHIFT], cotangent[:, :SHIFT]), "ctx", -1)
    residual = jnp.concatenate([image[:, SHIFT:], edge_image], axis=1)
    grad_top = jnp.concatenate([cotangent[:, SHIFT:], edge_grad], axis=1)
    edge_image, edge_grad = shifted((residual[:, :, :SHIFT], grad_top[:, :, :SHIFT]), "tp", -1)
    residual = to_padded(jnp.concatenate([residual[:, :, SHIFT:], edge_image], axis=2))
    grad_top = to_padded(jnp.concatenate([grad_top[:, :, SHIFT:], edge_grad], axis=2))
    tokens_all = residual.shape[0]
    windows = tokens_all // AREA

    grow = PAD - WIN
    index_pad = jnp.pad(
        bias_index.reshape(WIN, WIN, WIN, WIN), ((0, grow),) * 4, constant_values=-1
    ).reshape(-1)
    one_hot = index_pad[:, None] == jnp.arange(table_rows, dtype=jnp.int32)
    heads_all = table_whole.shape[0]
    rel_bias = jnp.einsum(
        "ht,qt->hq", table_whole, one_hot.astype(BF16), preferred_element_type=F32
    ).reshape(heads_all * AREA, AREA)
    key_spot = jnp.arange(AREA, dtype=jnp.int32)
    key_live = (key_spot // PAD < WIN) & (key_spot % PAD < WIN)
    rel_bias = jnp.where(key_live[None, :], rel_bias, ABSENT)
    col_start = lax.axis_index("tp") * columns
    region_here = lax.dynamic_slice_in_dim(regions, col_start, columns, 1)
    labels = to_padded(region_here[None]).reshape(windows // images, AREA)
    labels = jnp.concatenate([labels] * images, axis=0)
    mask_bias = jnp.where(labels[:, :, None] == labels[:, None, :], 0.0, MASKED).astype(F32)

    steps = tokens_all // ROWS
    sets = heads_all // GROUP
    half_steps = [steps] if steps < 2 else [steps // 2, steps - steps // 2]
    rows_full = jax.ShapeDtypeStruct((tokens_all, channels), F32)
    rows_all_half = jax.ShapeDtypeStruct((tokens_all, channels), BF16)
    prob_spec = pl.BlockSpec((PER_STEP, sets, TALL, AREA), lambda i: (i, 0, 0, 0))
    row = row_spec(channels)
    anywhere = pl.BlockSpec(memory_space=pl.ANY)
    dense = 2 * ROWS * channels * channels
    moved = ROWS * channels

    saved = []
    carried = ()
    for part, count in enumerate(half_steps):
        first = part * half_steps[0]
        placed = row_spec(channels, first)
        rows_half = jax.ShapeDtypeStruct((count * ROWS, channels), BF16)
        prob_shape = jax.ShapeDtypeStruct((count * PER_STEP, sets, TALL, AREA), F32)
        mask_spec = pl.BlockSpec((PER_STEP, AREA, AREA), lambda i, first=first: (i + first, 0, 0))
        mask_here = mask_bias
        if part:
            up_held, down_held, mask_here = lax.optimization_barrier((up_held, down_held, mask_bias))
        *kept, middle, normed_two = pl.pallas_call(
            forward_kernel,
            grid=(count,),
            in_specs=[
                placed, whole_spec(vec.shape), whole_spec(attn_w.shape), whole_spec(rel_bias.shape),
                mask_spec,
            ]
            + [anywhere] * len(carried),
            out_specs=[row, row, row, row, prob_spec, row, placed, placed],
            out_shape=[rows_half] * 4 + [prob_shape, rows_half, rows_full, rows_all_half],
            input_output_aliases={5 + n: 6 + n for n in range(len(carried))},
            cost_estimate=pl.CostEstimate(
                flops=40 * count * dense, bytes_accessed=20 * count * moved, transcendentals=0
            ),
            **PARAMS,
        )(residual, vec, attn_w, rel_bias, mask_here, *carried)
        carried = (middle, normed_two)
        saved.append(kept)

    up_w = gather_steps(up_held, last).reshape(channels, -1)
    down_w = gather_steps(down_held, last).reshape(channels, -1)
    ffn_all = up_w.shape[1]
    output_full, grad_mid, dffn, dupb, sums_two = pl.pallas_call(
        ffn_kernel,
        grid=(steps,),
        in_specs=[
            row, row, row, whole_spec(up_w.shape), whole_spec(down_w.shape),
            whole_spec(upb_whole.shape), whole_spec(vec.shape),
        ],
        out_specs=[
            row, row, whole_spec((2,) + up_w.shape), whole_spec((1, ffn_all)),
            whole_spec((8, channels)),
        ],
        out_shape=[
            rows_full, rows_full, jax.ShapeDtypeStruct((2,) + up_w.shape, F32), jax.ShapeDtypeStruct((1, ffn_all), F32),
            jax.ShapeDtypeStruct((8, channels), F32),
        ],
        scratch_shapes=[pltpu.VMEM((ROWS, channels), F32), pltpu.VMEM((ROWS, channels), F32)],
        cost_estimate=pl.CostEstimate(
            flops=60 * steps * dense, bytes_accessed=40 * steps * moved, transcendentals=0
        ),
        **PARAMS,
    )(middle, normed_two, grad_top, up_w, down_w, upb_whole, vec)
    across_high = across[::-1]
    ffn_total = joined(*first_halves([dffn]), "ctx", 1)
    orders = (across_high + near, near + across_high)

    weight_parts, score_parts, sum_parts = [], [], []
    carried = ()
    for part, count in enumerate(half_steps):
        first = part * half_steps[0]
        placed = row_spec(channels, first)
        gm_here = grad_mid
        if part:
            up_cut = halves(ffn_total[:1], *orders[0][0], ())
            down_cut = halves(ffn_total[1:], *orders[1][0], ())
            up_cut, down_cut, gm_here = lax.optimization_barrier((up_cut, down_cut, grad_mid))
            up_total = joined(*up_cut, *orders[0][0])
            down_total = joined(*down_cut, *orders[1][0])
            orders = (orders[0][1:], orders[1][1:])
        grad_full, dw, grad_score, sums_one = pl.pallas_call(
            backward_kernel,
            grid=(count,),
            in_specs=[
                placed, placed, row, row, row, row, prob_spec, row, whole_spec(attn_w.shape),
                whole_spec(vec.shape),
            ]
            + [anywhere] * len(carried),
            out_specs=[
                placed, whole_spec(attn_w.shape), whole_spec(rel_bias.shape),
                whole_spec((8, channels)),
            ],
            out_shape=[
                rows_full, jax.ShapeDtypeStruct(attn_w.shape, F32),
                jax.ShapeDtypeStruct(rel_bias.shape, F32),
                jax.ShapeDtypeStruct((8, channels), F32),
            ],
            input_output_aliases={10 + n: n for n in range(len(carried))},
            scratch_shapes=[
                pltpu.VMEM((ROWS, channels), BF16), pltpu.VMEM((3, ROWS, channels), BF16)
            ],
            cost_estimate=pl.CostEstimate(
                flops=60 * count * dense, bytes_accessed=40 * count * moved, transcendentals=0
            ),
            **PARAMS,
        )(residual, gm_here, *saved[part], attn_w, vec, *carried)
        carried = (grad_full,)
        weight_parts.append(dw)
        score_parts.append(grad_score)
        sum_parts.append(sums_one)
    if len(half_steps) == 1:
        up_total, down_total = ffn_total[:1], ffn_total[1:]
    else:
        up_total, down_total, weight_parts, score_parts, sum_parts, grad_full = (
            lax.optimization_barrier(
                (up_total, down_total, weight_parts, score_parts, sum_parts, grad_full)
            )
        )
    sums_one = sum(sum_parts)
    table_all = jnp.einsum(
        "hq,qt->ht",
        sum(score_parts).reshape(heads_all, AREA * AREA),
        one_hot.astype(F32),
        precision=lax.Precision.HIGHEST,
    )
    small_total = jnp.concatenate(
        [
            sums_one[:4].reshape(-1), sums_two[:4].reshape(-1), dupb.reshape(-1),
            table_all.reshape(-1),
        ]
    )
    small_plan = [(axis, bit) for axis in ("ctx", "tp", "fsdp") for bit in bits(axis)]
    attn_plan = [("ctx", 1)] + near + across_high + far
    up_plan, down_plan, ffn_plan = list(orders[0]), list(orders[1]), list(far)
    up_used = {bit for axis, bit in near if (axis, bit) not in up_plan}
    down_used = {bit for axis, bit in near if (axis, bit) not in down_plan}
    ffn_used = {bit for _, bit in near}
    attn_used = set()
    attn_sums, ffn_sums = None, None
    while attn_plan or small_plan or up_plan or down_plan or ffn_plan:
        if attn_plan:
            move = attn_plan.pop(0)
            if attn_sums is None:
                attn_sums = joined(*first_halves(weight_parts), *move)
            else:
                attn_sums = scatter_steps(attn_sums, [move], attn_used)
                attn_used |= {move[1]} if move[0] == "fsdp" else set()
        if small_plan:
            axis, bit = small_plan.pop(0)
            small_total = small_total + swap(small_total, axis, bit)
        if up_plan or down_plan:
            if up_plan:
                move = up_plan.pop(0)
                up_total = scatter_steps(up_total, [move], up_used)
                up_used |= {move[1]} if move[0] == "fsdp" else set()
            if down_plan:
                move = down_plan.pop(0)
                down_total = scatter_steps(down_total, [move], down_used)
                down_used |= {move[1]} if move[0] == "fsdp" else set()
            up_total, down_total, attn_sums, small_total = lax.optimization_barrier(
                (up_total, down_total, attn_sums, small_total)
            )
        else:
            if ffn_sums is None:
                ffn_sums = jnp.concatenate([up_total, down_total], axis=0)
            if ffn_plan:
                move = ffn_plan.pop(0)
                ffn_sums = scatter_steps(ffn_sums, [move], ffn_used)
                ffn_used.add(move[1])
            ffn_sums, attn_sums, small_total = lax.optimization_barrier(
                (ffn_sums, attn_sums, small_total)
            )
    if ffn_sums is None:
        ffn_sums = jnp.concatenate([up_total, down_total], axis=0)
    ffn_sums, attn_sums = ffn_sums[:, 0], attn_sums[:, 0]
    cut = 4 * channels
    one_sum = small_total[:cut].reshape(4, channels)
    two_sum = small_total[cut : 2 * cut].reshape(4, channels)
    upb_sum = small_total[2 * cut : 2 * cut + ffn_all]
    table_sum = small_total[2 * cut + ffn_all :].reshape(heads_all, table_rows)
    tp_index = lax.axis_index("tp")
    shard = lax.axis_index("fsdp") * lax.axis_size("ctx") + lax.axis_index("ctx")
    take = lambda value: lax.dynamic_slice_in_dim(value, shard * rows_here, rows_here, 1)
    gain_grad = take(jnp.stack([one_sum[2], two_sum[0]]))
    bias_grad = take(jnp.stack([one_sum[3], two_sum[1]]))
    out_grad = take(jnp.stack([two_sum[2], two_sum[3]]))
    qkv_bias_grad = lax.dynamic_slice_in_dim(one_sum[:2], tp_index * head_width, head_width, 1)
    up_bias_grad = lax.dynamic_slice_in_dim(upb_sum, tp_index * ffn_here, ffn_here, 0)
    table_grad = lax.dynamic_slice_in_dim(table_sum, tp_index * heads_here, heads_here, 0)

    output_full = from_padded(output_full, images, band_rows, columns)
    grad_full = from_padded(grad_full, images, band_rows, columns)
    edge_out, edge_back = shifted((output_full[:, :, -SHIFT:], grad_full[:, :, -SHIFT:]), "tp", 1)
    output_shift = jnp.concatenate([edge_out, output_full[:, :, :-SHIFT]], axis=2)
    grad_start = jnp.concatenate([edge_back, grad_full[:, :, :-SHIFT]], axis=2)
    edge_out, edge_back = shifted((output_shift[:, -SHIFT:], grad_start[:, -SHIFT:]), "ctx", 1)
    output = jnp.concatenate([edge_out, output_shift[:, :-SHIFT]], axis=1)
    image_grad = jnp.concatenate([edge_back, grad_start[:, :-SHIFT]], axis=1)
    return (
        output, image_grad, gain_grad, bias_grad,
        jnp.stack([attn_sums[0], attn_sums[1], attn_sums[2]], axis=1),
        qkv_bias_grad, table_grad, attn_sums[3].T, out_grad, ffn_sums[0], up_bias_grad,
        ffn_sums[1].T,
    )


def solution(mesh):
    in_specs = (
        P("fsdp", "ctx", "tp", None),
        P("fsdp", "ctx", "tp", None),
        P(None, ("fsdp", "ctx")),
        P(None, ("fsdp", "ctx")),
        P(("fsdp", "ctx"), None, "tp"),
        P(None, "tp"),
        P("tp", None),
        P(),
        P("ctx", None),
        P("tp", ("fsdp", "ctx")),
        P(None, ("fsdp", "ctx")),
        P(("fsdp", "ctx"), "tp"),
        P("tp"),
        P("tp", ("fsdp", "ctx")),
    )
    out_specs = (
        P("fsdp", "ctx", "tp", None),
        P("fsdp", "ctx", "tp", None),
        P(None, ("fsdp", "ctx")),
        P(None, ("fsdp", "ctx")),
        P(("fsdp", "ctx"), None, "tp"),
        P(None, "tp"),
        P("tp", None),
        P("tp", ("fsdp", "ctx")),
        P(None, ("fsdp", "ctx")),
        P(("fsdp", "ctx"), "tp"),
        P("tp"),
        P("tp", ("fsdp", "ctx")),
    )
    return jax.shard_map(
        per_device, mesh=mesh, in_specs=in_specs, out_specs=out_specs, check_vma=False
    )
```

profile of v0, /device:TPU:0, one launch (start us, length us, event | category | flops | bytes accessed | tf_op | source)
XLA Modules:
  0.0 245.8 jit_solution(11494786993573881017)
XLA Ops:
  2.2 4.0 %collective-permute-start.7 = (bf16[2,32,1024]{2,1,0:T(8,128)(2,1)}, bf16[2,32,1024]{2,1,0:T(8,128)(2,1)}, u32[]{:S(2)}, u32[]{:S(2)}) collective-permute-start(bf16[2,32,1024]{2,1,0:T(8,128)(2,1)} %pad_maximum_fusion.22), channel_id=1, source_target_pairs={{0,16},{4,20},{8,24},{12,28},{16,0},{20,4},{24,8},{28,12},{1,17},{... | collective-permute-start | bytes 393224 | tf_op jit(solution)/shard_map/ppermute | solution.py:40
  20.3 2.5 %slice.185 = f32[1,25,28,512]{3,0,2,1:T(1,128)S(1)} slice(f32[1,28,28,512]{3,0,2,1:T(1,128)} %param.14), slice={[0:1], [3:28], [0:28], [0:512]} | slice | bytes 2867200 | tf_op jit(solution)/shard_map/slice | solution.py:382
  32.8 2.7 %fusion.11 = f32[1,28,25,512]{3,0,2,1:T(1,128)S(1)} fusion(f32[1,25,28,512]{3,0,2,1:T(1,128)S(1)} %slice.185, f32[1,3,28,512]{3,0,2,1:T(1,128)} %collective-permute-done), kind=kLoop, calls=%fused_computation.27 | loop fusion | flops 358400 | bytes 3039232 | tf_op jit(solution)/shard_map/concatenate | solution.py:382
  37.5 2.1 fusion.10
  39.6 4.0 %collective-permute-done.4 = bf16[2,2,144,256]{3,2,1,0:T(8,128)(2,1)S(1)} collective-permute-done((bf16[2,2,144,256]{3,2,1,0:T(8,128)(2,1)S(1)}, bf16[2,2,144,256]{3,2,1,0:T(8,128)(2,1)S(1)}, u32[]{:S(2)}, u32[]{:S(2)}) %collective-permute-start.4) | collective-permute-done | bytes 294944 | tf_op jit(solution)/shard_map/ppermute | solution.py:40
  48.8 8.3 %collective-permute-done.5 = bf16[2,2,2,144,256]{4,3,2,1,0:T(8,128)(2,1)S(1)} collective-permute-done((bf16[2,2,2,144,256]{4,3,2,1,0:T(8,128)(2,1)S(1)}, bf16[2,2,2,144,256]{4,3,2,1,0:T(8,128)(2,1)S(1)}, u32[]{:S(2)}, u32[]{:S(2)}) %collective-permute-start.5) | collective-permute-done | bytes 589856 | tf_op jit(solution)/shard_map/ppermute | solution.py:40
  63.8 7.1 %collective-permute-done.9 = bf16[2,2,32,1024]{3,2,0,1:T(8,128)(2,1)S(1)} collective-permute-done((bf16[2,2,32,1024]{3,2,0,1:T(8,128)(2,1)S(1)}, bf16[2,2,32,1024]{3,2,0,1:T(8,128)(2,1)S(1)}, u32[]{:S(2)}, u32[]{:S(2)}) %collective-permute-start.9) | collective-permute-done | bytes 262176 | tf_op jit(solution)/shard_map/ppermute | solution.py:40
  83.4 10.4 %shard_map.229 = (bf16[512,512]{1,0:T(8,128)(2,1)}, bf16[512,512]{1,0:T(8,128)(2,1)}, bf16[512,512]{1,0:T(8,128)(2,1)}, bf16[512,512]{1,0:T(8,128)(2,1)}, f32[8,...) custom-call(f32[1024,512]{1,0:T(8,128)} %bitcast.233, ...), custom_call_target="tpu_custom_call" | custom-call | flops 10737418240 | bytes 5242880 | tf_op jit(solution)/shard_map/pallas_call | solution.py:430
  95.3 10.2 %shard_map.230 = (bf16[512,512]{1,0:T(8,128)(2,1)}, bf16[512,512]{1,0:T(8,128)(2,1)}, bf16[512,512]{1,0:T(8,128)(2,1)}, bf16[512,512]{1,0:T(8,128)(2,1)}, f32[8,...) custom-call(f32[1024,512]{1,0:T(8,128)} %bitcast.234, ...), custom_call_target="tpu_custom_call", output_to_operand_aliasing={{6}: (5, {}), {7}: (6, {})} | custom-call | flops 10737418240 | bytes 5242880 | tf_op jit(solution)/shard_map/pallas_call | solution.py:430
  110.3 26.8 %shard_map.231 = (f32[1024,512]{1,0:T(8,128)}, f32[1024,512]{1,0:T(8,128)}, f32[2,512,2048]{2,1,0:T(8,128)}, f32[1,2048]{1,0:T(1,128)}, f32[8,512]{1,0:T(8,128)}) custom-call(f32[1024,512]{1,0:T(8,128)} %get-tuple-element.83.mid_ref, bf16[1024,512]{1,0:T(8,128)(2,1)} %get-tuple-element.84.n2_ref, f32[1024,512]{1,0:T(8,128)} %bitcast.241, ...), custom_call_target="tpu_custom_call" | custom-call | flops 32212254720 | bytes 20971520 | tf_op jit(solution)/shard_map/pallas_call | solution.py:452
  137.1 2.5 %fusion.2 = bf16[2,8,32,2048]{3,2,1,0:T(8,128)(2,1)S(1)} fusion(f32[2,8,2,32,2048]{4,3,2,1,0:T(8,128)} %bitcast.223, s32[]{:T(128)S(6)} %select_n.389), kind=kLoop, calls=%fused_computation.6 | loop fusion | bytes 4194308 | tf_op jit(solution)/shard_map/convert_element_type | solution.py:76
  139.7 15.2 %shard_map.232 = (f32[1024,512]{1,0:T(8,128)}, f32[4,512,512]{2,1,0:T(8,128)}, f32[1024,64]{1,0:T(8,128)}, f32[8,512]{1,0:T(8,128)}) custom-call(f32[1024,512]{1,0:T(8,128)} %bitcast.235, f32[1024,512]{1,0:T(8,128)} %get-tuple-element.101.gm_ref, bf16[512,512]{1,0:T(8,128)(2,1)} %get-tuple-element.94.tok_ref, bf16[512,512]{1,0:T(8,128)(2,1)} %get-tuple-element.95.q_ref, ...), custom_call_target="tpu_custom_call" | custom-call | flops 16106127360 | bytes 10485760 | tf_op jit(solution)/shard_map/pallas_call | solution.py:490
  155.0 3.4 %bitcast_add_fusion = f32[2,8,32,2048]{3,2,1,0:T(8,128)S(1)} fusion(bf16[2,8,32,2048]{3,2,1,0:T(8,128)(2,1)} %collective-permute-done.19, f32[2,8,2,32,2048]{4,3,2,1,0:T(8,128)} %bitcast.224, s32[]{:T(128)S(6)} %select_n.388), kind=kLoop, calls=%fused_computation.1 | loop fusion | flops 2097152 | bytes 10485764 | tf_op jit(solution)/shard_map/add | solution.py:80
  160.9 15.4 %shard_map.233 = (f32[1024,512]{1,0:T(8,128)}, f32[4,512,512]{2,1,0:T(8,128)}, f32[1024,64]{1,0:T(8,128)}, f32[8,512]{1,0:T(8,128)}) custom-call(f32[1024,512]{1,0:T(8,128)} %bitcast.236, f32[1024,512]{1,0:T(8,128)} %get-tuple-element.101.gm_ref, bf16[512,512]{1,0:T(8,128)(2,1)} %get-tuple-element.102.tok_ref, ...), custom_call_target="tpu_custom_call", output_to_operand_aliasing={{0}: (10, {})} | custom-call | flops 16106127360 | bytes 10485760 | tf_op jit(solution)/shard_map/pallas_call | solution.py:490
  180.7 2.8 %fusion.12 = bf16[4,8,32,512]{3,2,1,0:T(8,128)(2,1)S(1)} fusion(f32[4,8,2,32,512]{4,3,2,1,0:T(8,128)} %bitcast.227, s32[]{:T(128)S(6)} %select_n.389, f32[4,8,2,32,512]{4,3,2,1,0:T(8,128)} %bitcast.225), kind=kLoop, calls=%fused_computation.31 | loop fusion | flops 1048576 | bytes 5242884 | tf_op jit(solution)/shard_map/convert_element_type | solution.py:76
  187.2 5.1 %collective-permute-done.25 = bf16[1,4,32,1024]{3,2,1,0:T(8,128)(2,1)S(1)} collective-permute-done((bf16[1,4,32,1024]{3,2,1,0:T(8,128)(2,1)S(1)}, bf16[1,4,32,1024]{3,2,1,0:T(8,128)(2,1)S(1)}, u32[]{:S(2)}, u32[]{:S(2)}) %collective-permute-start.25) | collective-permute-done | bytes 262176 | tf_op jit(solution)/shard_map/ppermute | solution.py:40
  197.6 2.6 %collective-permute-start.28 = (bf16[2,2,32,1024]{3,2,1,0:T(8,128)(2,1)}, bf16[2,2,32,1024]{3,2,1,0:T(8,128)(2,1)S(1)}, u32[]{:S(2)}, u32[]{:S(2)}) collective-permute-start(bf16[2,2,32,1024]{3,2,1,0:T(8,128)(2,1)} %fusion.15), channel_id=1, source_target_pairs={{0,16},{4,20},{8,24},{12,28},{16,0},{20,4},{24,8},{28,12},{1,17},{... | collective-permute-start | bytes 786440 | tf_op jit(solution)/shard_map/ppermute | solution.py:40
  206.6 4.5 %collective-permute-done.28 = bf16[2,2,32,1024]{3,2,1,0:T(8,128)(2,1)S(1)} collective-permute-done((bf16[2,2,32,1024]{3,2,1,0:T(8,128)(2,1)}, bf16[2,2,32,1024]{3,2,1,0:T(8,128)(2,1)S(1)}, u32[]{:S(2)}, u32[]{:S(2)}) %collective-permute-start.28) | collective-permute-done | bytes 262176 | tf_op jit(solution)/shard_map/ppermute | solution.py:40
  218.4 5.0 %collective-permute-done.32 = bf16[4,4,32,256]{3,2,1,0:T(8,128)(2,1)S(1)} collective-permute-done((bf16[4,4,32,256]{3,2,1,0:T(8,128)(2,1)S(1)}, bf16[4,4,32,256]{3,2,1,0:T(8,128)(2,1)S(1)}, u32[]{:S(2)}, u32[]{:S(2)}) %collective-permute-start.32) | collective-permute-done | bytes 262176 | tf_op jit(solution)/shard_map/ppermute | solution.py:40
  223.5 3.3 %collective-permute-start.34 = (bf16[4,2,32,256]{3,2,1,0:T(8,128)(2,1)S(1)}, bf16[4,2,32,256]{3,2,1,0:T(8,128)(2,1)S(1)}, u32[]{:S(2)}, u32[]{:S(2)}) collective-permute-start(bf16[4,2,32,256]{3,2,1,0:T(8,128)(2,1)S(1)} %fusion.20), channel_id=1, source_target_pairs={{0,16},{4,20},{8,24},{12,28},{16,0},{20,4},{24,8},{28,12},{1,17},{... | collective-permute-start | bytes 393224 | tf_op jit(solution)/shard_map/ppermute | solution.py:40
  226.8 2.5 %fusion.7 = f32[1,28,28,512]{3,0,2,1:T(1,128)} fusion(f32[1,28,25,512]{3,0,2,1:T(1,128)S(1)} %slice.256, f32[1,28,3,512]{3,0,2,1:T(1,128)S(1)} %collective-permute-done.17, f32[1,3,28,512]{3,0,2,1:T(1,128)S(1)} %collective-permute-done.18), kind=kLoop, calls=%fused_computation.17 | loop fusion | flops 802816 | bytes 3383296 | tf_op jit(solution)/shard_map/concatenate | solution.py:606
  230.9 3.8 %collective-permute-done.35 = f32[8848]{0:T(1024)S(1)} collective-permute-done((f32[8848]{0:T(1024)S(1)}, f32[8848]{0:T(1024)S(1)}, u32[]{:S(2)}, u32[]{:S(2)}) %collective-permute-start.35) | collective-permute-done | bytes 35424 | tf_op jit(solution)/shard_map/ppermute | solution.py:40
  235.0 2.5 %fusion.6 = f32[1,28,28,512]{3,0,2,1:T(1,128)} fusion(f32[1,28,25,512]{3,0,2,1:T(1,128)S(1)} %slice.261, f32[1,28,3,512]{3,0,2,1:T(1,128)S(1)} %collective-permute-done.22, f32[1,3,28,512]{3,0,2,1:T(1,128)S(1)} %collective-permute-done.23), kind=kLoop, calls=%fused_computation.15 | loop fusion | flops 802816 | bytes 3383296 | tf_op jit(solution)/shard_map/concatenate | solution.py:607
  237.5 2.1 collective-permute-done.37
  (241 shorter events, 94.7 us)
Async XLA Ops:
  2.2 26.2 %collective-permute-start.7 = (bf16[2,32,1024]{2,1,0:T(8,128)(2,1)}, bf16[2,32,1024]{2,1,0:T(8,128)(2,1)}, u32[]{:S(2)}, u32[]{:S(2)}) collective-permute-start(bf16[2,32,1024]{2,1,0:T(8,128)(2,1)} %pad_maximum_fusion.22), channel_id=1, source_target_pairs={{0,16},{4,20},{8,24},{12,28},{16,0},{20,4},{24,8},{28,12},{1,17},{... | collective-permute-start | bytes 393224 | tf_op jit(solution)/shard_map/ppermute | solution.py:40
  18.2 11.4 %collective-permute-start = (f32[1,3,28,512]{3,0,2,1:T(1,128)}, f32[1,3,28,512]{3,0,2,1:T(1,128)}, u32[]{:S(2)}, u32[]{:S(2)}) collective-permute-start(f32[1,3,28,512]{3,0,2,1:T(1,128)} %slice.186), channel_id=1, source_target_pairs={{0,2},{2,0},{1,3},{3,1},{4,6},{6,4},{5,7},{7,5},{8,10},{10,8},{9,1... | collective-permute-start | bytes 516104 | tf_op jit(solution)/shard_map/ppermute | solution.py:32
  19.8 12.6 %collective-permute-start.13 = (f32[1,3,28,512]{3,0,2,1:T(1,128)}, f32[1,3,28,512]{3,0,2,1:T(1,128)S(1)}, u32[]{:S(2)}, u32[]{:S(2)}) collective-permute-start(f32[1,3,28,512]{3,0,2,1:T(1,128)} %slice.201), channel_id=1, source_target_pairs={{0,2},{2,0},{1,3},{3,1},{4,6},{6,4},{5,7},{7,5},{8,10},{10,8},{9,1... | collective-permute-start | bytes 516104 | tf_op jit(solution)/shard_map/ppermute | solution.py:32
  29.4 17.7 %collective-permute-start.8 = (bf16[2,2,32,1024]{3,2,0,1:T(8,128)(2,1)S(1)}, bf16[2,2,32,1024]{3,2,0,1:T(8,128)(2,1)S(1)}, u32[]{:S(2)}, u32[]{:S(2)}) collective-permute-start(bf16[2,2,32,1024]{3,2,0,1:T(8,128)(2,1)S(1)} %pad_maximum_fusion.16), channel_id=1, source_target_pairs={{0,8},{4,12},{8,0},{12,4},{16,24},{20,28},{24,16},{28,20},{1,9},{5... | collective-permute-start | bytes 786440 | tf_op jit(solution)/shard_map/ppermute | solution.py:40
  30.5 14.9 %collective-permute-start.1 = (f32[1,28,3,512]{3,0,2,1:T(1,128)S(1)}, f32[1,28,3,512]{3,0,2,1:T(1,128)S(1)}, u32[]{:S(2)}, u32[]{:S(2)}) collective-permute-start(f32[1,28,3,512]{3,0,2,1:T(1,128)S(1)} %pad_maximum_fusion.20), channel_id=1, source_target_pairs={{0,1},{1,0},{2,3},{3,2},{4,5},{5,4},{6,7},{7,6},{8,9},{9,8},{10,11... | collective-permute-start | bytes 516104 | tf_op jit(solution)/shard_map/ppermute | solution.py:32
  32.5 24.9 %collective-permute-start.14 = (f32[1,28,3,512]{3,0,2,1:T(1,128)S(1)}, f32[1,28,3,512]{3,0,2,1:T(1,128)S(1)}, u32[]{:S(2)}, u32[]{:S(2)}) collective-permute-start(f32[1,28,3,512]{3,0,2,1:T(1,128)S(1)} %pad_maximum_fusion.19), channel_id=1, source_target_pairs={{0,1},{1,0},{2,3},{3,2},{4,5},{5,4},{6,7},{7,6},{8,9},{9,8},{10,11... | collective-permute-start | bytes 516104 | tf_op jit(solution)/shard_map/ppermute | solution.py:32
  43.7 13.4 %collective-permute-start.5 = (bf16[2,2,2,144,256]{4,3,2,1,0:T(8,128)(2,1)S(1)}, bf16[2,2,2,144,256]{4,3,2,1,0:T(8,128)(2,1)S(1)}, u32[]{:S(2)}, u32[]{:S(2)}) collective-permute-start(bf16[2,2,2,144,256]{4,3,2,1,0:T(8,128)(2,1)S(1)} %pad_maximum_fusion.11), channel_id=1, source_target_pairs={{0,1},{1,0},{2,3},{3,2},{4,5},{5,4},{6,7},{7,6},{8,9},{9,8},{10,11... | collective-permute-start | bytes 1769480 | tf_op jit(solution)/shard_map/ppermute | solution.py:40
  47.2 16.5 %collective-permute-start.10 = (bf16[2,2,32,1024]{3,2,0,1:T(8,128)(2,1)S(1)}, bf16[2,2,32,1024]{3,2,0,1:T(8,128)(2,1)S(1)}, u32[]{:S(2)}, u32[]{:S(2)}) collective-permute-start(bf16[2,2,32,1024]{3,2,0,1:T(8,128)(2,1)S(1)} %get-tuple-element.160), channel_id=1, source_target_pairs={{0,4},{4,0},{8,12},{12,8},{16,20},{20,16},{24,28},{28,24},{1,5},{5... | collective-permute-start | bytes 786440 | tf_op jit(solution)/shard_map/ppermute | solution.py:40
  57.4 13.7 %collective-permute-start.6 = (bf16[2,2,2,144,512]{4,3,2,1,0:T(8,128)(2,1)S(1)}, bf16[2,2,2,144,512]{4,3,2,1,0:T(8,128)(2,1)S(1)}, u32[]{:S(2)}, u32[]{:S(2)}) collective-permute-start(bf16[2,2,2,144,512]{4,3,2,1,0:T(8,128)(2,1)S(1)} %pad_maximum_fusion.7), channel_id=1, source_target_pairs={{0,2},{2,0},{1,3},{3,1},{4,6},{6,4},{5,7},{7,5},{8,10},{10,8},{9,1... | collective-permute-start | bytes 3538952 | tf_op jit(solution)/shard_map/ppermute | solution.py:40
  77.9 15.9 %collective-permute-start.12 = (bf16[2,2,2,32,1024]{4,3,0,1,2:T(8,128)(2,1)S(1)}, bf16[2,2,2,32,1024]{4,3,0,1,2:T(8,128)(2,1)S(1)}, u32[]{:S(2)}, u32[]{:S(2)}) collective-permute-start(bf16[2,2,2,32,1024]{4,3,0,1,2:T(8,128)(2,1)S(1)} %pad_maximum_fusion.13), channel_id=1, source_target_pairs={{0,1},{1,0},{2,3},{3,2},{4,5},{5,4},{6,7},{7,6},{8,9},{9,8},{10,11... | collective-permute-start | bytes 1572872 | tf_op jit(solution)/shard_map/ppermute | solution.py:40
  79.3 14.6 %collective-permute-start.11 = (bf16[2,2,32,2048]{3,2,0,1:T(8,128)(2,1)S(1)}, bf16[2,2,32,2048]{3,2,0,1:T(8,128)(2,1)S(1)}, u32[]{:S(2)}, u32[]{:S(2)}) collective-permute-start(bf16[2,2,32,2048]{3,2,0,1:T(8,128)(2,1)S(1)} %pad_maximum_fusion.12), channel_id=1, source_target_pairs={{0,4},{4,0},{8,12},{12,8},{16,20},{20,16},{24,28},{28,24},{1,5},{5... | collective-permute-start | bytes 1572872 | tf_op jit(solution)/shard_map/ppermute | solution.py:40
  94.1 11.4 %collective-permute-start.16 = (bf16[2,2,2,32,2048]{4,3,0,1,2:T(8,128)(2,1)S(1)}, bf16[2,2,2,32,2048]{4,3,0,1,2:T(8,128)(2,1)}, u32[]{:S(2)}, u32[]{:S(2)}) collective-permute-start(bf16[2,2,2,32,2048]{4,3,0,1,2:T(8,128)(2,1)S(1)} %get-tuple-element.86), channel_id=1, source_target_pairs={{0,2},{2,0},{1,3},{3,1},{4,6},{6,4},{5,7},{7,5},{8,10},{10,8},{9,1... | collective-permute-start | bytes 3145736 | tf_op jit(solution)/shard_map/ppermute | solution.py:40
  94.8 13.7 %collective-permute-start.15 = (bf16[2,2,2,32,2048]{4,3,0,1,2:T(8,128)(2,1)S(1)}, bf16[2,2,2,32,2048]{4,3,0,1,2:T(8,128)(2,1)S(1)}, u32[]{:S(2)}, u32[]{:S(2)}) collective-permute-start(bf16[2,2,2,32,2048]{4,3,0,1,2:T(8,128)(2,1)S(1)} %get-tuple-element.85), channel_id=1, source_target_pairs={{0,2},{2,0},{1,3},{3,1},{4,6},{6,4},{5,7},{7,5},{8,10},{10,8},{9,1... | collective-permute-start | bytes 3145736 | tf_op jit(solution)/shard_map/ppermute | solution.py:40
  139.6 15.4 %collective-permute-start.19 = (bf16[2,8,32,2048]{3,2,1,0:T(8,128)(2,1)S(1)}, bf16[2,8,32,2048]{3,2,1,0:T(8,128)(2,1)}, u32[]{:S(2)}, u32[]{:S(2)}) collective-permute-start(bf16[2,8,32,2048]{3,2,1,0:T(8,128)(2,1)S(1)} %fusion.2), channel_id=1, source_target_pairs={{0,2},{2,0},{1,3},{3,1},{4,6},{6,4},{5,7},{7,5},{8,10},{10,8},{9,1... | collective-permute-start | bytes 6291464 | tf_op jit(solution)/shard_map/ppermute | solution.py:40
  159.9 16.6 %collective-permute-start.21 = (bf16[1,4,32,2048]{3,2,1,0:T(8,128)(2,1)S(1)}, bf16[1,4,32,2048]{3,2,1,0:T(8,128)(2,1)}, u32[]{:S(2)}, u32[]{:S(2)}) collective-permute-start(bf16[1,4,32,2048]{3,2,1,0:T(8,128)(2,1)S(1)} %fusion.13), channel_id=1, source_target_pairs={{0,4},{4,0},{8,12},{12,8},{16,20},{20,16},{24,28},{28,24},{1,5},{5... | collective-permute-start | bytes 1572872 | tf_op jit(solution)/shard_map/ppermute | solution.py:40
  160.4 17.3 %collective-permute-start.20 = (bf16[1,8,32,1024]{3,2,1,0:T(8,128)(2,1)}, bf16[1,8,32,1024]{3,2,1,0:T(8,128)(2,1)S(1)}, u32[]{:S(2)}, u32[]{:S(2)}) collective-permute-start(bf16[1,8,32,1024]{3,2,1,0:T(8,128)(2,1)} %dynamic-slice_convert_fusion.2), channel_id=1, source_target_pairs={{0,1},{1,0},{2,3},{3,2},{4,5},{5,4},{6,7},{7,6},{8,9},{9,8},{10,11... | collective-permute-start | bytes 1572872 | tf_op jit(solution)/shard_map/ppermute | solution.py:40
  183.5 10.3 %collective-permute-start.26 = (bf16[4,8,32,512]{3,2,1,0:T(8,128)(2,1)S(1)}, bf16[4,8,32,512]{3,2,1,0:T(8,128)(2,1)S(1)}, u32[]{:S(2)}, u32[]{:S(2)}) collective-permute-start(bf16[4,8,32,512]{3,2,1,0:T(8,128)(2,1)S(1)} %fusion.12), channel_id=1, source_target_pairs={{0,2},{2,0},{1,3},{3,1},{4,6},{6,4},{5,7},{7,5},{8,10},{10,8},{9,1... | collective-permute-start | bytes 3145736 | tf_op jit(solution)/shard_map/ppermute | solution.py:40
  195.2 15.9 %collective-permute-start.29 = (bf16[4,4,32,512]{3,2,1,0:T(8,128)(2,1)}, bf16[4,4,32,512]{3,2,1,0:T(8,128)(2,1)}, u32[]{:S(2)}, u32[]{:S(2)}) collective-permute-start(bf16[4,4,32,512]{3,2,1,0:T(8,128)(2,1)} %fusion.14), channel_id=1, source_target_pairs={{0,4},{4,0},{8,12},{12,8},{16,20},{20,16},{24,28},{28,24},{1,5},{5... | collective-permute-start | bytes 1572872 | tf_op jit(solution)/shard_map/ppermute | solution.py:40
  197.6 13.5 %collective-permute-start.28 = (bf16[2,2,32,1024]{3,2,1,0:T(8,128)(2,1)}, bf16[2,2,32,1024]{3,2,1,0:T(8,128)(2,1)S(1)}, u32[]{:S(2)}, u32[]{:S(2)}) collective-permute-start(bf16[2,2,32,1024]{3,2,1,0:T(8,128)(2,1)} %fusion.15), channel_id=1, source_target_pairs={{0,16},{4,20},{8,24},{12,28},{16,0},{20,4},{24,8},{28,12},{1,17},{... | collective-permute-start | bytes 786440 | tf_op jit(solution)/shard_map/ppermute | solution.py:40
  205.1 9.6 %collective-permute-start.17 = (f32[1,28,3,512]{3,0,2,1:T(1,128)S(1)}, f32[1,28,3,512]{3,0,2,1:T(1,128)S(1)}, u32[]{:S(2)}, u32[]{:S(2)}) collective-permute-start(f32[1,28,3,512]{3,0,2,1:T(1,128)S(1)} %slice.255), channel_id=1, source_target_pairs={{0,1},{1,0},{2,3},{3,2},{4,5},{5,4},{6,7},{7,6},{8,9},{9,8},{10,11... | collective-permute-start | bytes 516104 | tf_op jit(solution)/shard_map/ppermute | solution.py:32
  214.0 9.3 %collective-permute-start.32 = (bf16[4,4,32,256]{3,2,1,0:T(8,128)(2,1)S(1)}, bf16[4,4,32,256]{3,2,1,0:T(8,128)(2,1)S(1)}, u32[]{:S(2)}, u32[]{:S(2)}) collective-permute-start(bf16[4,4,32,256]{3,2,1,0:T(8,128)(2,1)S(1)} %dynamic-slice_convert_fusion.3), channel_id=1, source_target_pairs={{0,1},{1,0},{2,3},{3,2},{4,5},{5,4},{6,7},{7,6},{8,9},{9,8},{10,11... | collective-permute-start | bytes 786440 | tf_op jit(solution)/shard_map/ppermute | solution.py:40
  214.8 12.0 %collective-permute-start.18 = (f32[1,3,28,512]{3,0,2,1:T(1,128)S(1)}, f32[1,3,28,512]{3,0,2,1:T(1,128)S(1)}, u32[]{:S(2)}, u32[]{:S(2)}) collective-permute-start(f32[1,3,28,512]{3,0,2,1:T(1,128)S(1)} %pad_maximum_fusion.18), channel_id=1, source_target_pairs={{0,2},{2,0},{1,3},{3,1},{4,6},{6,4},{5,7},{7,5},{8,10},{10,8},{9,1... | collective-permute-start | bytes 516104 | tf_op jit(solution)/shard_map/ppermute | solution.py:32
  216.8 13.8 %collective-permute-start.22 = (f32[1,28,3,512]{3,0,2,1:T(1,128)S(1)}, f32[1,28,3,512]{3,0,2,1:T(1,128)S(1)}, u32[]{:S(2)}, u32[]{:S(2)}) collective-permute-start(f32[1,28,3,512]{3,0,2,1:T(1,128)S(1)} %slice.260), channel_id=1, source_target_pairs={{0,1},{1,0},{2,3},{3,2},{4,5},{5,4},{6,7},{7,6},{8,9},{9,8},{10,11... | collective-permute-start | bytes 516104 | tf_op jit(solution)/shard_map/ppermute | solution.py:32
  223.5 11.2 %collective-permute-start.34 = (bf16[4,2,32,256]{3,2,1,0:T(8,128)(2,1)S(1)}, bf16[4,2,32,256]{3,2,1,0:T(8,128)(2,1)S(1)}, u32[]{:S(2)}, u32[]{:S(2)}) collective-permute-start(bf16[4,2,32,256]{3,2,1,0:T(8,128)(2,1)S(1)} %fusion.20), channel_id=1, source_target_pairs={{0,16},{4,20},{8,24},{12,28},{16,0},{20,4},{24,8},{28,12},{1,17},{... | collective-permute-start | bytes 393224 | tf_op jit(solution)/shard_map/ppermute | solution.py:40
  (28 other events, 182.3 us)
where the time goes:
time: 250 us; the launch traced here: 246 us
  Pallas kernels  78 us (31%)
  local copies, waits for them, and re-layouts  47.9 us (19%)
  waiting for transfers between devices  41.3 us (17%)
  starting transfers between devices  37.6 us (15%)
  other arithmetic  36.9 us (15%)
    ppermute x30, waiting for transfers between devices, swap(): lax.ppermute(value, axis, [(i, i ^ bit) for i in range(lax.axis_size(axis...  41.3 us
    ppermute x30, starting transfers between devices, swap(): lax.ppermute(value, axis, [(i, i ^ bit) for i in range(lax.axis_size(axis...  31.7 us
    pallas_call x2, Pallas kernels, per_device(): pl.pallas_call(backward_kernel, grid=(count,), in_specs=[placed, placed,...  30.7 us
    pallas_call x1, Pallas kernels, per_device(): pl.pallas_call(ffn_kernel, grid=(steps,), in_specs=[row, row, row, whole_...  26.8 us
    pallas_call x2, Pallas kernels, per_device(): pl.pallas_call(forward_kernel, grid=(count,), in_specs=[placed, whole_spe...  20.6 us
    add x12, other arithmetic, joined(): return keep + swap(send, axis, bit).astype(F32)  8.05 us
    unnamed x39, local copies, waits for them, and re-layouts  6.69 us
    ppermute x8, starting transfers between devices, shifted(): return lax.ppermute(value, axis, pairs)  5.87 us
  transfers between devices with their start and end apart: 38, of which 9 were waited for; matrix products, arithmetic and copies ran while one was open for 24% of the time, Pallas kernels for 21%

commit v1 on v0

--- a/solution.py
+++ b/solution.py
@@ -216,7 +216,7 @@
         dupb_ref[:, here] += jnp.sum(slope, axis=0, keepdims=True)
         return carry
 
-    lax.fori_loop(0, up_ref.shape[1] // chunk, step, 0)
+    lax.fori_loop(0, up_ref.shape[1] // chunk, step, 0, unroll=True)
     middle = mid_ref[...]
     cot = cot_ref[...]
     out_ref[...] = middle + acc_ref[...] + vec[5:6]

time: 250 us -> 247 us (0.988)
  Pallas kernels: 78 us -> 74.8 us
    pallas_call x1, Pallas kernels: 26.8 us -> 23.4 us  [per_device(): pl.pallas_call(ffn_kernel, grid=(steps,), in_specs=[row, row, row, whole_...]
where the time goes in v1:
time: 247 us; the launch traced here: 243 us
  Pallas kernels  74.8 us (30%)
  local copies, waits for them, and re-layouts  47.9 us (19%)
  waiting for transfers between devices  41.3 us (17%)
  starting transfers between devices  37.6 us (15%)
  other arithmetic  36.9 us (15%)
    ppermute x30, waiting for transfers between devices, swap(): lax.ppermute(value, axis, [(i, i ^ bit) for i in range(lax.axis_size(axis...  41.3 us
    ppermute x30, starting transfers between devices, swap(): lax.ppermute(value, axis, [(i, i ^ bit) for i in range(lax.axis_size(axis...  31.7 us
    pallas_call x2, Pallas kernels, per_device(): pl.pallas_call(backward_kernel, grid=(count,), in_specs=[placed, placed,...  31.1 us
    pallas_call x1, Pallas kernels, per_device(): pl.pallas_call(ffn_kernel, grid=(steps,), in_specs=[row, row, row, whole_...  23.4 us
    pallas_call x2, Pallas kernels, per_device(): pl.pallas_call(forward_kernel, grid=(count,), in_specs=[placed, whole_spe...  20.4 us
    add x12, other arithmetic, joined(): return keep + swap(send, axis, bit).astype(F32)  8.05 us
    unnamed x39, local copies, waits for them, and re-layouts  6.69 us
    ppermute x8, starting transfers between devices, shifted(): return lax.ppermute(value, axis, pairs)  5.9 us
  transfers between devices with their start and end apart: 38, of which 9 were waited for; matrix products, arithmetic and copies ran while one was open for 24% of the time, Pallas kernels for 21%

profile of v1, /device:TPU:0, one launch (start us, length us, event | category | flops | bytes accessed | tf_op | source)
XLA Modules:
  0.0 242.6 jit_solution(14085489508197071355)
XLA Ops:
  2.2 4.0 %collective-permute-start.7 = (bf16[2,32,1024]{2,1,0:T(8,128)(2,1)}, bf16[2,32,1024]{2,1,0:T(8,128)(2,1)}, u32[]{:S(2)}, u32[]{:S(2)}) collective-permute-start(bf16[2,32,1024]{2,1,0:T(8,128)(2,1)} %pad_maximum_fusion.22), channel_id=1, source_target_pairs={{0,16},{4,20},{8,24},{12,28},{16,0},{20,4},{24,8},{28,12},{1,17},{... | collective-permute-start | bytes 393224 | tf_op jit(solution)/shard_map/ppermute | solution.py:40
  20.3 2.5 %slice.185 = f32[1,25,28,512]{3,0,2,1:T(1,128)S(1)} slice(f32[1,28,28,512]{3,0,2,1:T(1,128)} %param.14), slice={[0:1], [3:28], [0:28], [0:512]} | slice | bytes 2867200 | tf_op jit(solution)/shard_map/slice | solution.py:382
  32.8 2.7 %fusion.11 = f32[1,28,25,512]{3,0,2,1:T(1,128)S(1)} fusion(f32[1,25,28,512]{3,0,2,1:T(1,128)S(1)} %slice.185, f32[1,3,28,512]{3,0,2,1:T(1,128)} %collective-permute-done), kind=kLoop, calls=%fused_computation.27 | loop fusion | flops 358400 | bytes 3039232 | tf_op jit(solution)/shard_map/concatenate | solution.py:382
  37.5 2.1 fusion.10
  39.6 4.0 %collective-permute-done.4 = bf16[2,2,144,256]{3,2,1,0:T(8,128)(2,1)S(1)} collective-permute-done((bf16[2,2,144,256]{3,2,1,0:T(8,128)(2,1)S(1)}, bf16[2,2,144,256]{3,2,1,0:T(8,128)(2,1)S(1)}, u32[]{:S(2)}, u32[]{:S(2)}) %collective-permute-start.4) | collective-permute-done | bytes 294944 | tf_op jit(solution)/shard_map/ppermute | solution.py:40
  48.8 8.3 %collective-permute-done.5 = bf16[2,2,2,144,256]{4,3,2,1,0:T(8,128)(2,1)S(1)} collective-permute-done((bf16[2,2,2,144,256]{4,3,2,1,0:T(8,128)(2,1)S(1)}, bf16[2,2,2,144,256]{4,3,2,1,0:T(8,128)(2,1)S(1)}, u32[]{:S(2)}, u32[]{:S(2)}) %collective-permute-start.5) | collective-permute-done | bytes 589856 | tf_op jit(solution)/shard_map/ppermute | solution.py:40
  63.8 7.1 %collective-permute-done.9 = bf16[2,2,32,1024]{3,2,0,1:T(8,128)(2,1)S(1)} collective-permute-done((bf16[2,2,32,1024]{3,2,0,1:T(8,128)(2,1)S(1)}, bf16[2,2,32,1024]{3,2,0,1:T(8,128)(2,1)S(1)}, u32[]{:S(2)}, u32[]{:S(2)}) %collective-permute-start.9) | collective-permute-done | bytes 262176 | tf_op jit(solution)/shard_map/ppermute | solution.py:40
  83.4 10.2 %shard_map.229 = (bf16[512,512]{1,0:T(8,128)(2,1)}, bf16[512,512]{1,0:T(8,128)(2,1)}, bf16[512,512]{1,0:T(8,128)(2,1)}, bf16[512,512]{1,0:T(8,128)(2,1)}, f32[8,...) custom-call(f32[1024,512]{1,0:T(8,128)} %bitcast.233, ...), custom_call_target="tpu_custom_call" | custom-call | flops 10737418240 | bytes 5242880 | tf_op jit(solution)/shard_map/pallas_call | solution.py:430
  95.1 10.2 %shard_map.230 = (bf16[512,512]{1,0:T(8,128)(2,1)}, bf16[512,512]{1,0:T(8,128)(2,1)}, bf16[512,512]{1,0:T(8,128)(2,1)}, bf16[512,512]{1,0:T(8,128)(2,1)}, f32[8,...) custom-call(f32[1024,512]{1,0:T(8,128)} %bitcast.234, ...), custom_call_target="tpu_custom_call", output_to_operand_aliasing={{6}: (5, {}), {7}: (6, {})} | custom-call | flops 10737418240 | bytes 5242880 | tf_op jit(solution)/shard_map/pallas_call | solution.py:430
  110.1 23.4 %shard_map.231 = (f32[1024,512]{1,0:T(8,128)}, f32[1024,512]{1,0:T(8,128)}, f32[2,512,2048]{2,1,0:T(8,128)}, f32[1,2048]{1,0:T(1,128)}, f32[8,512]{1,0:T(8,128)}) custom-call(f32[1024,512]{1,0:T(8,128)} %get-tuple-element.83.mid_ref, bf16[1024,512]{1,0:T(8,128)(2,1)} %get-tuple-element.84.n2_ref, f32[1024,512]{1,0:T(8,128)} %bitcast.241, ...), custom_call_target="tpu_custom_call" | custom-call | flops 32212254720 | bytes 20971520 | tf_op jit(solution)/shard_map/pallas_call | solution.py:452
  133.4 2.5 %fusion.2 = bf16[2,8,32,2048]{3,2,1,0:T(8,128)(2,1)S(1)} fusion(f32[2,8,2,32,2048]{4,3,2,1,0:T(8,128)} %bitcast.223, s32[]{:T(128)S(6)} %select_n.389), kind=kLoop, calls=%fused_computation.6 | loop fusion | bytes 4194308 | tf_op jit(solution)/shard_map/convert_element_type | solution.py:76
  136.1 15.7 %shard_map.232 = (f32[1024,512]{1,0:T(8,128)}, f32[4,512,512]{2,1,0:T(8,128)}, f32[1024,64]{1,0:T(8,128)}, f32[8,512]{1,0:T(8,128)}) custom-call(f32[1024,512]{1,0:T(8,128)} %bitcast.235, f32[1024,512]{1,0:T(8,128)} %get-tuple-element.101.gm_ref, bf16[512,512]{1,0:T(8,128)(2,1)} %get-tuple-element.94.tok_ref, bf16[512,512]{1,0:T(8,128)(2,1)} %get-tuple-element.95.q_ref, ...), custom_call_target="tpu_custom_call" | custom-call | flops 16106127360 | bytes 10485760 | tf_op jit(solution)/shard_map/pallas_call | solution.py:490
  151.8 3.4 %bitcast_add_fusion = f32[2,8,32,2048]{3,2,1,0:T(8,128)S(1)} fusion(bf16[2,8,32,2048]{3,2,1,0:T(8,128)(2,1)} %collective-permute-done.19, f32[2,8,2,32,2048]{4,3,2,1,0:T(8,128)} %bitcast.224, s32[]{:T(128)S(6)} %select_n.388), kind=kLoop, calls=%fused_computation.1 | loop fusion | flops 2097152 | bytes 10485764 | tf_op jit(solution)/shard_map/add | solution.py:80
  157.8 15.4 %shard_map.233 = (f32[1024,512]{1,0:T(8,128)}, f32[4,512,512]{2,1,0:T(8,128)}, f32[1024,64]{1,0:T(8,128)}, f32[8,512]{1,0:T(8,128)}) custom-call(f32[1024,512]{1,0:T(8,128)} %bitcast.236, f32[1024,512]{1,0:T(8,128)} %get-tuple-element.101.gm_ref, bf16[512,512]{1,0:T(8,128)(2,1)} %get-tuple-element.102.tok_ref, ...), custom_call_target="tpu_custom_call", output_to_operand_aliasing={{0}: (10, {})} | custom-call | flops 16106127360 | bytes 10485760 | tf_op jit(solution)/shard_map/pallas_call | solution.py:490
  177.6 2.8 %fusion.12 = bf16[4,8,32,512]{3,2,1,0:T(8,128)(2,1)S(1)} fusion(f32[4,8,2,32,512]{4,3,2,1,0:T(8,128)} %bitcast.227, s32[]{:T(128)S(6)} %select_n.389, f32[4,8,2,32,512]{4,3,2,1,0:T(8,128)} %bitcast.225), kind=kLoop, calls=%fused_computation.31 | loop fusion | flops 1048576 | bytes 5242884 | tf_op jit(solution)/shard_map/convert_element_type | solution.py:76
  184.1 5.2 %collective-permute-done.25 = bf16[1,4,32,1024]{3,2,1,0:T(8,128)(2,1)S(1)} collective-permute-done((bf16[1,4,32,1024]{3,2,1,0:T(8,128)(2,1)S(1)}, bf16[1,4,32,1024]{3,2,1,0:T(8,128)(2,1)S(1)}, u32[]{:S(2)}, u32[]{:S(2)}) %collective-permute-start.25) | collective-permute-done | bytes 262176 | tf_op jit(solution)/shard_map/ppermute | solution.py:40
  194.4 2.6 %collective-permute-start.28 = (bf16[2,2,32,1024]{3,2,1,0:T(8,128)(2,1)}, bf16[2,2,32,1024]{3,2,1,0:T(8,128)(2,1)S(1)}, u32[]{:S(2)}, u32[]{:S(2)}) collective-permute-start(bf16[2,2,32,1024]{3,2,1,0:T(8,128)(2,1)} %fusion.15), channel_id=1, source_target_pairs={{0,16},{4,20},{8,24},{12,28},{16,0},{20,4},{24,8},{28,12},{1,17},{... | collective-permute-start | bytes 786440 | tf_op jit(solution)/shard_map/ppermute | solution.py:40
  203.5 4.5 %collective-permute-done.28 = bf16[2,2,32,1024]{3,2,1,0:T(8,128)(2,1)S(1)} collective-permute-done((bf16[2,2,32,1024]{3,2,1,0:T(8,128)(2,1)}, bf16[2,2,32,1024]{3,2,1,0:T(8,128)(2,1)S(1)}, u32[]{:S(2)}, u32[]{:S(2)}) %collective-permute-start.28) | collective-permute-done | bytes 262176 | tf_op jit(solution)/shard_map/ppermute | solution.py:40
  215.2 5.0 %collective-permute-done.32 = bf16[4,4,32,256]{3,2,1,0:T(8,128)(2,1)S(1)} collective-permute-done((bf16[4,4,32,256]{3,2,1,0:T(8,128)(2,1)S(1)}, bf16[4,4,32,256]{3,2,1,0:T(8,128)(2,1)S(1)}, u32[]{:S(2)}, u32[]{:S(2)}) %collective-permute-start.32) | collective-permute-done | bytes 262176 | tf_op jit(solution)/shard_map/ppermute | solution.py:40
  220.3 3.3 %collective-permute-start.34 = (bf16[4,2,32,256]{3,2,1,0:T(8,128)(2,1)S(1)}, bf16[4,2,32,256]{3,2,1,0:T(8,128)(2,1)S(1)}, u32[]{:S(2)}, u32[]{:S(2)}) collective-permute-start(bf16[4,2,32,256]{3,2,1,0:T(8,128)(2,1)S(1)} %fusion.20), channel_id=1, source_target_pairs={{0,16},{4,20},{8,24},{12,28},{16,0},{20,4},{24,8},{28,12},{1,17},{... | collective-permute-start | bytes 393224 | tf_op jit(solution)/shard_map/ppermute | solution.py:40
  223.7 2.5 %fusion.7 = f32[1,28,28,512]{3,0,2,1:T(1,128)} fusion(f32[1,28,25,512]{3,0,2,1:T(1,128)S(1)} %slice.256, f32[1,28,3,512]{3,0,2,1:T(1,128)S(1)} %collective-permute-done.17, f32[1,3,28,512]{3,0,2,1:T(1,128)S(1)} %collective-permute-done.18), kind=kLoop, calls=%fused_computation.17 | loop fusion | flops 802816 | bytes 3383296 | tf_op jit(solution)/shard_map/concatenate | solution.py:606
  227.7 3.8 %collective-permute-done.35 = f32[8848]{0:T(1024)S(1)} collective-permute-done((f32[8848]{0:T(1024)S(1)}, f32[8848]{0:T(1024)S(1)}, u32[]{:S(2)}, u32[]{:S(2)}) %collective-permute-start.35) | collective-permute-done | bytes 35424 | tf_op jit(solution)/shard_map/ppermute | solution.py:40
  231.9 2.5 %fusion.6 = f32[1,28,28,512]{3,0,2,1:T(1,128)} fusion(f32[1,28,25,512]{3,0,2,1:T(1,128)S(1)} %slice.261, f32[1,28,3,512]{3,0,2,1:T(1,128)S(1)} %collective-permute-done.22, f32[1,3,28,512]{3,0,2,1:T(1,128)S(1)} %collective-permute-done.23), kind=kLoop, calls=%fused_computation.15 | loop fusion | flops 802816 | bytes 3383296 | tf_op jit(solution)/shard_map/concatenate | solution.py:607
  234.4 2.1 collective-permute-done.37
  (241 shorter events, 94.7 us)
Async XLA Ops:
  2.2 26.2 %collective-permute-start.7 = (bf16[2,32,1024]{2,1,0:T(8,128)(2,1)}, bf16[2,32,1024]{2,1,0:T(8,128)(2,1)}, u32[]{:S(2)}, u32[]{:S(2)}) collective-permute-start(bf16[2,32,1024]{2,1,0:T(8,128)(2,1)} %pad_maximum_fusion.22), channel_id=1, source_target_pairs={{0,16},{4,20},{8,24},{12,28},{16,0},{20,4},{24,8},{28,12},{1,17},{... | collective-permute-start | bytes 393224 | tf_op jit(solution)/shard_map/ppermute | solution.py:40
  18.2 11.4 %collective-permute-start = (f32[1,3,28,512]{3,0,2,1:T(1,128)}, f32[1,3,28,512]{3,0,2,1:T(1,128)}, u32[]{:S(2)}, u32[]{:S(2)}) collective-permute-start(f32[1,3,28,512]{3,0,2,1:T(1,128)} %slice.186), channel_id=1, source_target_pairs={{0,2},{2,0},{1,3},{3,1},{4,6},{6,4},{5,7},{7,5},{8,10},{10,8},{9,1... | collective-permute-start | bytes 516104 | tf_op jit(solution)/shard_map/ppermute | solution.py:32
  19.8 12.6 %collective-permute-start.13 = (f32[1,3,28,512]{3,0,2,1:T(1,128)}, f32[1,3,28,512]{3,0,2,1:T(1,128)S(1)}, u32[]{:S(2)}, u32[]{:S(2)}) collective-permute-start(f32[1,3,28,512]{3,0,2,1:T(1,128)} %slice.201), channel_id=1, source_target_pairs={{0,2},{2,0},{1,3},{3,1},{4,6},{6,4},{5,7},{7,5},{8,10},{10,8},{9,1... | collective-permute-start | bytes 516104 | tf_op jit(solution)/shard_map/ppermute | solution.py:32
  29.4 17.7 %collective-permute-start.8 = (bf16[2,2,32,1024]{3,2,0,1:T(8,128)(2,1)S(1)}, bf16[2,2,32,1024]{3,2,0,1:T(8,128)(2,1)S(1)}, u32[]{:S(2)}, u32[]{:S(2)}) collective-permute-start(bf16[2,2,32,1024]{3,2,0,1:T(8,128)(2,1)S(1)} %pad_maximum_fusion.16), channel_id=1, source_target_pairs={{0,8},{4,12},{8,0},{12,4},{16,24},{20,28},{24,16},{28,20},{1,9},{5... | collective-permute-start | bytes 786440 | tf_op jit(solution)/shard_map/ppermute | solution.py:40
  30.5 14.9 %collective-permute-start.1 = (f32[1,28,3,512]{3,0,2,1:T(1,128)S(1)}, f32[1,28,3,512]{3,0,2,1:T(1,128)S(1)}, u32[]{:S(2)}, u32[]{:S(2)}) collective-permute-start(f32[1,28,3,512]{3,0,2,1:T(1,128)S(1)} %pad_maximum_fusion.20), channel_id=1, source_target_pairs={{0,1},{1,0},{2,3},{3,2},{4,5},{5,4},{6,7},{7,6},{8,9},{9,8},{10,11... | collective-permute-start | bytes 516104 | tf_op jit(solution)/shard_map/ppermute | solution.py:32
  32.5 24.9 %collective-permute-start.14 = (f32[1,28,3,512]{3,0,2,1:T(1,128)S(1)}, f32[1,28,3,512]{3,0,2,1:T(1,128)S(1)}, u32[]{:S(2)}, u32[]{:S(2)}) collective-permute-start(f32[1,28,3,512]{3,0,2,1:T(1,128)S(1)} %pad_maximum_fusion.19), channel_id=1, source_target_pairs={{0,1},{1,0},{2,3},{3,2},{4,5},{5,4},{6,7},{7,6},{8,9},{9,8},{10,11... | collective-permute-start | bytes 516104 | tf_op jit(solution)/shard_map/ppermute | solution.py:32
  43.7 13.4 %collective-permute-start.5 = (bf16[2,2,2,144,256]{4,3,2,1,0:T(8,128)(2,1)S(1)}, bf16[2,2,2,144,256]{4,3,2,1,0:T(8,128)(2,1)S(1)}, u32[]{:S(2)}, u32[]{:S(2)}) collective-permute-start(bf16[2,2,2,144,256]{4,3,2,1,0:T(8,128)(2,1)S(1)} %pad_maximum_fusion.11), channel_id=1, source_target_pairs={{0,1},{1,0},{2,3},{3,2},{4,5},{5,4},{6,7},{7,6},{8,9},{9,8},{10,11... | collective-permute-start | bytes 1769480 | tf_op jit(solution)/shard_map/ppermute | solution.py:40
  47.2 16.5 %collective-permute-start.10 = (bf16[2,2,32,1024]{3,2,0,1:T(8,128)(2,1)S(1)}, bf16[2,2,32,1024]{3,2,0,1:T(8,128)(2,1)S(1)}, u32[]{:S(2)}, u32[]{:S(2)}) collective-permute-start(bf16[2,2,32,1024]{3,2,0,1:T(8,128)(2,1)S(1)} %get-tuple-element.160), channel_id=1, source_target_pairs={{0,4},{4,0},{8,12},{12,8},{16,20},{20,16},{24,28},{28,24},{1,5},{5... | collective-permute-start | bytes 786440 | tf_op jit(solution)/shard_map/ppermute | solution.py:40
  57.4 13.7 %collective-permute-start.6 = (bf16[2,2,2,144,512]{4,3,2,1,0:T(8,128)(2,1)S(1)}, bf16[2,2,2,144,512]{4,3,2,1,0:T(8,128)(2,1)S(1)}, u32[]{:S(2)}, u32[]{:S(2)}) collective-permute-start(bf16[2,2,2,144,512]{4,3,2,1,0:T(8,128)(2,1)S(1)} %pad_maximum_fusion.7), channel_id=1, source_target_pairs={{0,2},{2,0},{1,3},{3,1},{4,6},{6,4},{5,7},{7,5},{8,10},{10,8},{9,1... | collective-permute-start | bytes 3538952 | tf_op jit(solution)/shard_map/ppermute | solution.py:40
  77.9 15.7 %collective-permute-start.12 = (bf16[2,2,2,32,1024]{4,3,0,1,2:T(8,128)(2,1)S(1)}, bf16[2,2,2,32,1024]{4,3,0,1,2:T(8,128)(2,1)S(1)}, u32[]{:S(2)}, u32[]{:S(2)}) collective-permute-start(bf16[2,2,2,32,1024]{4,3,0,1,2:T(8,128)(2,1)S(1)} %pad_maximum_fusion.13), channel_id=1, source_target_pairs={{0,1},{1,0},{2,3},{3,2},{4,5},{5,4},{6,7},{7,6},{8,9},{9,8},{10,11... | collective-permute-start | bytes 1572872 | tf_op jit(solution)/shard_map/ppermute | solution.py:40
  79.3 14.4 %collective-permute-start.11 = (bf16[2,2,32,2048]{3,2,0,1:T(8,128)(2,1)S(1)}, bf16[2,2,32,2048]{3,2,0,1:T(8,128)(2,1)S(1)}, u32[]{:S(2)}, u32[]{:S(2)}) collective-permute-start(bf16[2,2,32,2048]{3,2,0,1:T(8,128)(2,1)S(1)} %pad_maximum_fusion.12), channel_id=1, source_target_pairs={{0,4},{4,0},{8,12},{12,8},{16,20},{20,16},{24,28},{28,24},{1,5},{5... | collective-permute-start | bytes 1572872 | tf_op jit(solution)/shard_map/ppermute | solution.py:40
  93.9 11.4 %collective-permute-start.16 = (bf16[2,2,2,32,2048]{4,3,0,1,2:T(8,128)(2,1)S(1)}, bf16[2,2,2,32,2048]{4,3,0,1,2:T(8,128)(2,1)}, u32[]{:S(2)}, u32[]{:S(2)}) collective-permute-start(bf16[2,2,2,32,2048]{4,3,0,1,2:T(8,128)(2,1)S(1)} %get-tuple-element.86), channel_id=1, source_target_pairs={{0,2},{2,0},{1,3},{3,1},{4,6},{6,4},{5,7},{7,5},{8,10},{10,8},{9,1... | collective-permute-start | bytes 3145736 | tf_op jit(solution)/shard_map/ppermute | solution.py:40
  94.6 13.7 %collective-permute-start.15 = (bf16[2,2,2,32,2048]{4,3,0,1,2:T(8,128)(2,1)S(1)}, bf16[2,2,2,32,2048]{4,3,0,1,2:T(8,128)(2,1)S(1)}, u32[]{:S(2)}, u32[]{:S(2)}) collective-permute-start(bf16[2,2,2,32,2048]{4,3,0,1,2:T(8,128)(2,1)S(1)} %get-tuple-element.85), channel_id=1, source_target_pairs={{0,2},{2,0},{1,3},{3,1},{4,6},{6,4},{5,7},{7,5},{8,10},{10,8},{9,1... | collective-permute-start | bytes 3145736 | tf_op jit(solution)/shard_map/ppermute | solution.py:40
  135.9 15.8 %collective-permute-start.19 = (bf16[2,8,32,2048]{3,2,1,0:T(8,128)(2,1)S(1)}, bf16[2,8,32,2048]{3,2,1,0:T(8,128)(2,1)}, u32[]{:S(2)}, u32[]{:S(2)}) collective-permute-start(bf16[2,8,32,2048]{3,2,1,0:T(8,128)(2,1)S(1)} %fusion.2), channel_id=1, source_target_pairs={{0,2},{2,0},{1,3},{3,1},{4,6},{6,4},{5,7},{7,5},{8,10},{10,8},{9,1... | collective-permute-start | bytes 6291464 | tf_op jit(solution)/shard_map/ppermute | solution.py:40
  156.7 16.6 %collective-permute-start.21 = (bf16[1,4,32,2048]{3,2,1,0:T(8,128)(2,1)S(1)}, bf16[1,4,32,2048]{3,2,1,0:T(8,128)(2,1)}, u32[]{:S(2)}, u32[]{:S(2)}) collective-permute-start(bf16[1,4,32,2048]{3,2,1,0:T(8,128)(2,1)S(1)} %fusion.13), channel_id=1, source_target_pairs={{0,4},{4,0},{8,12},{12,8},{16,20},{20,16},{24,28},{28,24},{1,5},{5... | collective-permute-start | bytes 1572872 | tf_op jit(solution)/shard_map/ppermute | solution.py:40
  157.2 17.3 %collective-permute-start.20 = (bf16[1,8,32,1024]{3,2,1,0:T(8,128)(2,1)}, bf16[1,8,32,1024]{3,2,1,0:T(8,128)(2,1)S(1)}, u32[]{:S(2)}, u32[]{:S(2)}) collective-permute-start(bf16[1,8,32,1024]{3,2,1,0:T(8,128)(2,1)} %dynamic-slice_convert_fusion.2), channel_id=1, source_target_pairs={{0,1},{1,0},{2,3},{3,2},{4,5},{5,4},{6,7},{7,6},{8,9},{9,8},{10,11... | collective-permute-start | bytes 1572872 | tf_op jit(solution)/shard_map/ppermute | solution.py:40
  180.4 10.2 %collective-permute-start.26 = (bf16[4,8,32,512]{3,2,1,0:T(8,128)(2,1)S(1)}, bf16[4,8,32,512]{3,2,1,0:T(8,128)(2,1)S(1)}, u32[]{:S(2)}, u32[]{:S(2)}) collective-permute-start(bf16[4,8,32,512]{3,2,1,0:T(8,128)(2,1)S(1)} %fusion.12), channel_id=1, source_target_pairs={{0,2},{2,0},{1,3},{3,1},{4,6},{6,4},{5,7},{7,5},{8,10},{10,8},{9,1... | collective-permute-start | bytes 3145736 | tf_op jit(solution)/shard_map/ppermute | solution.py:40
  192.1 15.9 %collective-permute-start.29 = (bf16[4,4,32,512]{3,2,1,0:T(8,128)(2,1)}, bf16[4,4,32,512]{3,2,1,0:T(8,128)(2,1)}, u32[]{:S(2)}, u32[]{:S(2)}) collective-permute-start(bf16[4,4,32,512]{3,2,1,0:T(8,128)(2,1)} %fusion.14), channel_id=1, source_target_pairs={{0,4},{4,0},{8,12},{12,8},{16,20},{20,16},{24,28},{28,24},{1,5},{5... | collective-permute-start | bytes 1572872 | tf_op jit(solution)/shard_map/ppermute | solution.py:40
  194.4 13.5 %collective-permute-start.28 = (bf16[2,2,32,1024]{3,2,1,0:T(8,128)(2,1)}, bf16[2,2,32,1024]{3,2,1,0:T(8,128)(2,1)S(1)}, u32[]{:S(2)}, u32[]{:S(2)}) collective-permute-start(bf16[2,2,32,1024]{3,2,1,0:T(8,128)(2,1)} %fusion.15), channel_id=1, source_target_pairs={{0,16},{4,20},{8,24},{12,28},{16,0},{20,4},{24,8},{28,12},{1,17},{... | collective-permute-start | bytes 786440 | tf_op jit(solution)/shard_map/ppermute | solution.py:40
  201.9 9.6 %collective-permute-start.17 = (f32[1,28,3,512]{3,0,2,1:T(1,128)S(1)}, f32[1,28,3,512]{3,0,2,1:T(1,128)S(1)}, u32[]{:S(2)}, u32[]{:S(2)}) collective-permute-start(f32[1,28,3,512]{3,0,2,1:T(1,128)S(1)} %slice.255), channel_id=1, source_target_pairs={{0,1},{1,0},{2,3},{3,2},{4,5},{5,4},{6,7},{7,6},{8,9},{9,8},{10,11... | collective-permute-start | bytes 516104 | tf_op jit(solution)/shard_map/ppermute | solution.py:32
  210.9 9.3 %collective-permute-start.32 = (bf16[4,4,32,256]{3,2,1,0:T(8,128)(2,1)S(1)}, bf16[4,4,32,256]{3,2,1,0:T(8,128)(2,1)S(1)}, u32[]{:S(2)}, u32[]{:S(2)}) collective-permute-start(bf16[4,4,32,256]{3,2,1,0:T(8,128)(2,1)S(1)} %dynamic-slice_convert_fusion.3), channel_id=1, source_target_pairs={{0,1},{1,0},{2,3},{3,2},{4,5},{5,4},{6,7},{7,6},{8,9},{9,8},{10,11... | collective-permute-start | bytes 786440 | tf_op jit(solution)/shard_map/ppermute | solution.py:40
  211.7 12.0 %collective-permute-start.18 = (f32[1,3,28,512]{3,0,2,1:T(1,128)S(1)}, f32[1,3,28,512]{3,0,2,1:T(1,128)S(1)}, u32[]{:S(2)}, u32[]{:S(2)}) collective-permute-start(f32[1,3,28,512]{3,0,2,1:T(1,128)S(1)} %pad_maximum_fusion.18), channel_id=1, source_target_pairs={{0,2},{2,0},{1,3},{3,1},{4,6},{6,4},{5,7},{7,5},{8,10},{10,8},{9,1... | collective-permute-start | bytes 516104 | tf_op jit(solution)/shard_map/ppermute | solution.py:32
  213.6 13.8 %collective-permute-start.22 = (f32[1,28,3,512]{3,0,2,1:T(1,128)S(1)}, f32[1,28,3,512]{3,0,2,1:T(1,128)S(1)}, u32[]{:S(2)}, u32[]{:S(2)}) collective-permute-start(f32[1,28,3,512]{3,0,2,1:T(1,128)S(1)} %slice.260), channel_id=1, source_target_pairs={{0,1},{1,0},{2,3},{3,2},{4,5},{5,4},{6,7},{7,6},{8,9},{9,8},{10,11... | collective-permute-start | bytes 516104 | tf_op jit(solution)/shard_map/ppermute | solution.py:32
  220.3 11.2 %collective-permute-start.34 = (bf16[4,2,32,256]{3,2,1,0:T(8,128)(2,1)S(1)}, bf16[4,2,32,256]{3,2,1,0:T(8,128)(2,1)S(1)}, u32[]{:S(2)}, u32[]{:S(2)}) collective-permute-start(bf16[4,2,32,256]{3,2,1,0:T(8,128)(2,1)S(1)} %fusion.20), channel_id=1, source_target_pairs={{0,16},{4,20},{8,24},{12,28},{16,0},{20,4},{24,8},{28,12},{1,17},{... | collective-permute-start | bytes 393224 | tf_op jit(solution)/shard_map/ppermute | solution.py:40
  (28 other events, 182.3 us)
